TPU v7x, 32 devices: a whole 2x2x4 slice. The times are simulated.
32 devices in a mesh: dom: 8 (over z, y), sub: 4 (over x, core).
Axes of the slice: x: 2, y: 2, z: 4, core: 2. Of those that a mesh axis runs over, the one named last changes fastest.
Arguments:
- history: bfloat16 [32768, 256], P(('dom', 'sub')), may hold values from -140 to 140
- tile_weight: bfloat16 [256, 64, 128, 128], P(('dom', 'sub')), may hold values from 0 to 1.75, as said below
- tile_source: int32 [256, 64], P(('dom', 'sub')), may hold values from 0 to 63
- tile_live: int32 [256], P(('dom', 'sub')), may hold values from 8 to 64, as said below
- send_list: int32 [32, 8, 4], P(('dom', 'sub')), may hold values from 0 to 7
- degree: int32 [32768], P(('dom', 'sub')), may hold values from 16 to 64
- labels: int32 [32768], P(('dom', 'sub')), may hold values from 0 to 171
- neigh_weight: bfloat16 [256, 172], replicated, may hold values from -0.375 to 0.375
- self_weight: bfloat16 [256, 172], replicated, may hold values from -0.375 to 0.375
Outputs:
- grad_history: float32 [32768, 256], P(('dom', 'sub'))
- neigh_grad: float32 [256, 172], replicated
- self_grad: float32 [256, 172], replicated
Inputs may be any that keep to these rules, and one draw needn't show every extreme that they name: `tile_live`: every device owns a block with all 64 tiles live. `tile_weight`: nonzero entries lie within 0.25 and 1.75.
All inputs are finite; a program needn't handle non-finite values.
Results may differ from a plain program's by a relative error of at most 0.0055.
Values may be sent and summed in bfloat16 or wider, within the bound.
A program may use at most 192 MiB of HBM per device.

v0:
```python
import jax
import jax.numpy as jnp
from jax import lax
from jax.sharding import PartitionSpec as P


def per_device(
    history,
    tile_weight,
    tile_source,
    tile_live,
    send_list,
    degree,
    labels,
    neigh_weight,
    self_weight,
):
    block_count = tile_weight.shape[0]
    tile_slots = tile_weight.shape[1]
    block_rows = tile_weight.shape[2]
    width = history.shape[1]
    classes = neigh_weight.shape[1]
    dom_count = lax.axis_size("dom")
    nodes_all = history.shape[0] * dom_count * lax.axis_size("sub")
    own_blocks = history.reshape(block_count, block_rows, width)
    partition = lax.all_gather(own_blocks, "sub", axis=0, tiled=True)
    part_blocks = partition.shape[0]
    own_ids = jnp.arange(block_count, dtype=jnp.int32)
    send_table = send_list[0][:, :, None] == own_ids[None, None, :]
    outgoing = jnp.einsum(
        "pks,sif->pkif",
        send_table.astype(jnp.bfloat16),
        own_blocks,
        preferred_element_type=jnp.float32,
    ).astype(jnp.bfloat16)
    boundary = lax.all_to_all(outgoing, "dom", split_axis=0, concat_axis=0, tiled=True)
    slot_count = boundary.shape[1]
    sources = jnp.concatenate(
        [partition, boundary.reshape(dom_count * slot_count, block_rows, width)], axis=0
    )
    source_total = sources.shape[0]
    live_mask = jnp.arange(tile_slots, dtype=jnp.int32)[None, :] < tile_live[:, None]
    source_ids = jnp.arange(source_total, dtype=jnp.int32)
    picker = (tile_source[:, :, None] == source_ids[None, None, :]) & live_mask[:, :, None]
    picker_half = picker.astype(jnp.bfloat16)
    gathered = jnp.einsum(
        "bts,sjf->btjf", picker_half, sources, preferred_element_type=jnp.float32
    ).astype(jnp.bfloat16)
    summed = jnp.einsum("btij,btjf->bif", tile_weight, gathered, preferred_element_type=jnp.float32)
    degrees = degree.astype(jnp.float32)
    aggregate = (
        (summed / degrees.reshape(block_count, block_rows)[:, :, None])
        .astype(jnp.bfloat16)
        .reshape(-1, width)
    )
    logits = jnp.dot(aggregate, neigh_weight, preferred_element_type=jnp.float32) + jnp.dot(
        history, self_weight, preferred_element_type=jnp.float32
    )
    predicted = jax.nn.softmax(logits, axis=-1)
    onehot = (labels[:, None] == jnp.arange(classes, dtype=jnp.int32)[None, :]).astype(jnp.float32)
    residual = predicted - onehot
    delta = residual.astype(jnp.bfloat16)
    neigh_part = jnp.einsum("nf,nc->fc", aggregate, delta, preferred_element_type=jnp.float32)
    self_part = jnp.einsum("nf,nc->fc", history, delta, preferred_element_type=jnp.float32)
    neigh_total, self_total = lax.psum((neigh_part, self_part), ("dom", "sub"))
    norm_factor = float(nodes_all) ** (-0.5)
    scaled = (
        (residual / degrees[:, None]).astype(jnp.bfloat16).reshape(block_count, block_rows, classes)
    )
    per_tile = jnp.einsum("btij,bic->btjc", tile_weight, scaled, preferred_element_type=jnp.float32)
    by_source = jnp.einsum(
        "bts,btjc->sjc", picker.astype(jnp.float32), per_tile, precision=lax.Precision.HIGHEST
    )
    local_part = by_source[:part_blocks]
    boundary_grad = by_source[part_blocks:].reshape(dom_count, slot_count, block_rows, classes)
    local_grad = lax.psum_scatter(
        local_part.astype(jnp.bfloat16), "sub", scatter_dimension=0, tiled=True
    ).astype(jnp.float32)
    neigh_float = neigh_weight.astype(jnp.float32)
    return_table = send_table.astype(jnp.float32)
    boundary_features = jnp.einsum(
        "skic,fc->skif", boundary_grad, neigh_float, precision=lax.Precision.HIGHEST
    )
    arrived = lax.all_to_all(
        boundary_features.astype(jnp.bfloat16), "dom", split_axis=0, concat_axis=0, tiled=True
    ).astype(boundary_features.dtype)
    incoming = jnp.einsum("pks,pkif->sif", return_table, arrived, precision=lax.Precision.HIGHEST)
    neigh_term = jnp.dot(
        local_grad.reshape(-1, classes), neigh_float.T, precision=lax.Precision.HIGHEST
    ) + incoming.reshape(-1, width)
    grad_history = neigh_term + jnp.dot(delta, self_weight.T, preferred_element_type=jnp.float32)
    return (grad_history, neigh_total * norm_factor, self_total * norm_factor)


def solution(mesh):
    placed = (
        P(("dom", "sub"), None),
        P(("dom", "sub"), None, None, None),
        P(("dom", "sub"), None),
        P(("dom", "sub")),
        P(("dom", "sub"), None, None),
        P(("dom", "sub")),
        P(("dom", "sub")),
        P(),
        P(),
    )
    return jax.shard_map(
        per_device,
        mesh=mesh,
        in_specs=placed,
        out_specs=(P(("dom", "sub"), None), P(), P()),
        check_vma=False,
    )
```

profile of v0, /device:TPU:1, one launch (start us, length us, event | category | flops | bytes accessed | tf_op | source)
XLA Modules:
  0.0 383.9 jit_solution(7695579908305104222)
XLA Ops:
  7.2 1.8 convolution_convert_fusion.1
  9.0 1.8 copy.21
  10.8 6.4 %all-to-all-start = ((bf16[8,4,128,256]{3,2,1,0:T(8,128)(2,1)}), bf16[8,4,128,256]{3,2,1,0:T(8,128)(2,1)S(1)}, u32[]{:S(2)}, u32[]{:S(2)}) async-start(bf16[8,4,128,256]{3,2,1,0:T(8,128)(2,1)} %copy.21), calls=%async_computation | async-start | bytes 4194304 | tf_op jit(solution)/shard_map/all_to_all | solution.py:36
  17.3 0.7 all-gather.2.cloned.1.call-update
  18.0 22.9 %copy.35 = bf16[8,64,128,128]{2,1,3,0:T(8,128)(2,1)} copy(bf16[8,64,128,128]{3,2,1,0:T(8,128)(2,1)} %param.10) | data formatting | bytes 33554432 | tf_op args[1]
  40.9 3.4 all-gather.2.cloned.1.call-done
  44.3 4.1 %copy.22 = bf16[32,128,256]{2,0,1:T(8,128)(2,1)} copy(bf16[32,128,256]{2,1,0:T(8,128)(2,1)} %all-gather.2.cloned.1.call-done) | data formatting | bytes 4194304 | tf_op jit(solution)/shard_map/all_gather | solution.py:26
  48.4 16.2 %all-to-all-done = bf16[8,4,128,256]{3,2,1,0:T(8,128)(2,1)S(1)} async-done(((bf16[8,4,128,256]{3,2,1,0:T(8,128)(2,1)}), bf16[8,4,128,256]{3,2,1,0:T(8,128)(2,1)S(1)}, u32[]{:S(2)}, u32[]{:S(2)}) %all-to-all-start) | async-done | bytes 2097184 | tf_op jit(solution)/shard_map/all_to_all | solution.py:36
  64.6 2.5 copy.23
  67.1 17.8 %fusion.24 = bf16[8,256,128]{1,2,0:T(8,128)(2,1)S(1)} fusion(bf16[8,64,128,128]{2,1,3,0:T(8,128)(2,1)} %copy.35, bf16[32,128,256]{2,0,1:T(8,128)(2,1)} %copy.23, bf16[32,128,256]{2,0,1:T(8,128)(2,1)} %copy.22, f32[8,128]{1,0:T(8,128)S(1)} %get-tuple-element.7, s32[8,64]{1,0:T(8,128)S(1)} %copy-done.8, pred[8,64]{1,0:T(8,128)(4,1)S(1)} %iota_compare_fusion.3), kind=kOutput, calls=%fused_computation.23 | convolution fusion | flops 6468206592 | bytes 21502464 | tf_op jit(solution)/shard_map/btij,btjf->bif/dot_general | solution.py:49
  85.8 1.0 fusion.43
  86.8 23.6 %convolution_bitcast_fusion = f32[8,64,128,172]{2,3,1,0:T(8,128)} fusion(bf16[8,64,128,128]{3,2,1,0:T(8,128)(2,1)} %param.10, bf16[8,128,172,1]{1,0,2,3:T(8,128)(2,1)S(1)} %bitcast_bitcast_fusion), kind=kOutput, calls=%fused_computation.5 | convolution fusion | flops 2885681152 | bytes 62218240 | tf_op jit(solution)/shard_map/btij,bic->btjc/dot_general | solution.py:70
  110.5 62.0 %fusion.10 = f32[64,128,172]{1,0,2:T(8,128)S(1)} fusion(f32[8,64,128,172]{2,3,1,0:T(8,128)} %convolution_bitcast_fusion, s32[8,64]{1,0:T(8,128)S(1)} %copy-done.8, pred[8,64]{1,0:T(8,128)(4,1)S(1)} %iota_compare_fusion.3), kind=kOutput, calls=%fused_computation.10 | convolution fusion | flops 8657108992 | bytes 50727424 | tf_op jit(solution)/shard_map/bts,btjc->sjc/dot_general | solution.py:71
  172.5 2.4 copy-done.1
  174.9 0.4 slice.10
  175.3 5.8 %copy.28 = f32[8,4,128,172]{3,0,1,2:T(8,128)} copy(f32[8,4,128,172]{2,1,0,3:T(4,128)S(1)} %bitcast.97) | data formatting | bytes 5636096 | tf_op jit(solution)/shard_map/reshape | solution.py:75
  181.0 4.3 %convolution_convert_fusion = bf16[8,4,128,256]{3,0,1,2:T(8,128)(2,1)S(1)} fusion(f32[8,4,128,172]{3,0,1,2:T(8,128)} %copy.28, bf16[256,172]{0,1:T(8,128)(2,1)S(1)} %copy-done), kind=kOutput, calls=%fused_computation.13 | convolution fusion | flops 2165309440 | bytes 5003264 | tf_op jit(solution)/shard_map/skic,fc->skif/dot_general | solution.py:81
  185.3 2.1 copy.29
  187.5 4.7 %all-to-all-start.1 = ((bf16[8,4,128,256]{3,1,2,0:T(4,128)(2,1)}), bf16[8,4,128,256]{3,1,2,0:T(4,128)(2,1)S(1)}, u32[]{:S(2)}, u32[]{:S(2)}) async-start(bf16[8,4,128,256]{3,1,2,0:T(4,128)(2,1)} %copy.29), calls=%async_computation.1 | async-start | bytes 4194304 | tf_op jit(solution)/shard_map/all_to_all | solution.py:84
  192.2 2.0 fusion.55
  194.2 0.9 convolution_bitcast_fusion.1
  195.2 2.1 slice.14
  197.3 0.5 copy.46
  197.9 1.5 copy.67
  199.4 143.5 %all-reduce.3.cloned.1.call-done = (f32[256,172]{0,1:T(8,128)}, f32[256,172]{0,1:T(8,128)}) async-done(((f32[256,172]{0,1:T(8,128)}, f32[256,172]{0,1:T(8,128)}), (f32[256,172]{0,1:T(8,128)}, f32[256,172]{0,1:T(8,128)})) %all-reduce.3.cloned.1.call-update) | async-done | bytes 352272 | tf_op jit(solution)/shard_map/psum | solution.py:65
  342.9 1.8 broadcast_multiply_fusion
  344.7 27.9 %reduce-scatter.4.cloned.1.call-done = bf16[8,22016]{1,0:T(8,128)(2,1)} async-done(((bf16[32,22016]{1,0:T(8,128)(2,1)}), bf16[8,22016]{1,0:T(8,128)(2,1)}) %reduce-scatter.4.cloned.1.call-update) | async-done | bytes 352272
  372.6 1.2 reshape.74
  374.0 1.3 fusion.15
  375.3 0.3 copy.31
  375.7 0.4 convolution_add_fusion.1
  376.1 1.3 convolution_add_fusion
  (37 shorter events, 1.3 us)
Async XLA Ops:
  7.2 77.8 %copy-start = (bf16[256,172]{0,1:T(8,128)(2,1)S(1)}, bf16[256,172]{0,1:T(8,128)(2,1)}, u32[]{:S(2)}) copy-start(bf16[256,172]{0,1:T(8,128)(2,1)} %param.16) | copy-start | bytes 264196
  10.8 53.8 %all-to-all-start = ((bf16[8,4,128,256]{3,2,1,0:T(8,128)(2,1)}), bf16[8,4,128,256]{3,2,1,0:T(8,128)(2,1)S(1)}, u32[]{:S(2)}, u32[]{:S(2)}) async-start(bf16[8,4,128,256]{3,2,1,0:T(8,128)(2,1)} %copy.21), calls=%async_computation | async-start | bytes 4194304 | tf_op jit(solution)/shard_map/all_to_all | solution.py:36
  17.2 27.1 %all-gather.2.cloned.1.call-start = ((), (), s32[]{:S(2)}) async-start(), calls=%async_computation.3 | async-start | bytes 2621440 | tf_op jit(solution)/shard_map/all_gather | solution.py:26
  18.0 22.9 %copy-start.10 = (s32[8]{0:T(128)S(1)}, s32[8]{0:T(128)}, u32[]{:S(2)}) copy-start(s32[8]{0:T(128)} %param.12) | copy-start | bytes 100
  18.0 23.0 %copy-start.9 = (s32[1024]{0:T(1024)S(1)}, s32[1024]{0:T(1024)}, u32[]{:S(2)}) copy-start(s32[1024]{0:T(1024)} %param.14) | copy-start | bytes 12292
  40.9 26.2 %copy-start.8 = (s32[8,64]{1,0:T(8,128)S(1)}, s32[8,64]{1,0:T(8,128)}, u32[]{:S(2)}) copy-start(s32[8,64]{1,0:T(8,128)} %param.11) | copy-start | bytes 6148
  67.1 18.1 %copy-start.2 = (bf16[1024,256]{1,0:T(8,128)(2,1)S(1)}, bf16[1024,256]{1,0:T(8,128)(2,1)}, u32[]{:S(2)}) copy-start(bf16[1024,256]{1,0:T(8,128)(2,1)} %param.9) | copy-start | bytes 1572868
  67.1 18.1 %copy-start.5 = (bf16[256,172]{0,1:T(8,128)(2,1)S(1)}, bf16[256,172]{0,1:T(8,128)(2,1)}, u32[]{:S(2)}) copy-start(bf16[256,172]{0,1:T(8,128)(2,1)} %param.17) | copy-start | bytes 264196
  67.1 18.6 %copy-start.7 = (s32[1024]{0:T(1024)S(1)}, s32[1024]{0:T(1024)}, u32[]{:S(2)}) copy-start(s32[1024]{0:T(1024)} %param.15) | copy-start | bytes 12292
  84.9 25.5 %copy-start.4 = (bf16[8,256,128]{1,2,0:T(8,128)(2,1)}, bf16[8,256,128]{1,2,0:T(8,128)(2,1)S(1)}, u32[]{:S(2)}) copy-start(bf16[8,256,128]{1,2,0:T(8,128)(2,1)S(1)} %fusion.24) | copy-start | bytes 1572868
  172.4 2.4 copy-start.1
  185.3 6.9 %copy-start.3 = (bf16[1024,172]{0,1:T(8,128)(2,1)S(1)}, bf16[1024,172]{0,1:T(8,128)(2,1)}, u32[]{:S(2)}) copy-start(bf16[1024,172]{0,1:T(8,128)(2,1)} %get-tuple-element.5) | copy-start | bytes 1056772
  187.5 186.5 %all-to-all-start.1 = ((bf16[8,4,128,256]{3,1,2,0:T(4,128)(2,1)}), bf16[8,4,128,256]{3,1,2,0:T(4,128)(2,1)S(1)}, u32[]{:S(2)}, u32[]{:S(2)}) async-start(bf16[8,4,128,256]{3,1,2,0:T(4,128)(2,1)} %copy.29), calls=%async_computation.1 | async-start | bytes 4194304 | tf_op jit(solution)/shard_map/all_to_all | solution.py:84
  192.1 150.8 %all-reduce.3.cloned.1.call-start = ((), (), s32[]{:S(2)}) async-start(), calls=%async_computation.5 | async-start | bytes 720896 | tf_op jit(solution)/shard_map/psum | solution.py:65
  195.1 177.5 %reduce-scatter.4.cloned.1.call-start = ((), (), s32[]{:S(2)}) async-start(), calls=%async_computation.4 | async-start | bytes 1761280
  197.9 176.1 %copy-start.6 = (s32[1,8,4]{1,2,0:T(4,128)S(1)}, s32[1,8,4]{1,2,0:T(4,128)}, u32[]{:S(2)}) copy-start(s32[1,8,4]{1,2,0:T(4,128)} %param.13) | copy-start | bytes 388
Sparse Core Ops, SparseCore 0:
  19.6 24.6 all-gather.1
  199.0 143.8 all-reduce.2
  345.6 26.9 reduce-scatter.3
where the time goes:
time: 386 us; the launch traced here: 384 us
  waiting for transfers between devices  192 us (50%)
  matrix products  116 us (30%)
  local copies, waits for them, and re-layouts  48 us (12%)
  between operations  14 us (4%)
  starting transfers between devices  11.2 us (3%)
    psum x1, waiting for transfers between devices, per_device(): neigh_total, self_total = lax.psum((neigh_part, self_part), ('dom', 'sub'))  144 us
    dot_general x1, matrix products, per_device(): jnp.einsum('bts,btjc->sjc', picker.astype(jnp.float32), per_tile, precisi...  62 us
    unnamed x30, local copies, waits for them, and re-layouts  28.8 us
    unnamed x4, waiting for transfers between devices  28.7 us
    dot_general x1, matrix products, per_device(): jnp.einsum('btij,bic->btjc', tile_weight, scaled, preferred_element_type=...  23.6 us
    dot_general x1, matrix products, per_device(): jnp.einsum('btij,btjf->bif', tile_weight, gathered, preferred_element_typ...  17.8 us
    all_to_all x1, waiting for transfers between devices, per_device(): lax.all_to_all(outgoing, 'dom', split_axis=0, concat_axis=0, tiled=True)  16.2 us
  transfers between devices with their start and end apart: 5, of which 4 were waited for; matrix products, arithmetic and copies ran while one was open for 10% of the time, Pallas kernels for 0%

commit v1 on v0

v1 whole, which is shorter than its diff:
```python
import functools

import jax
import jax.numpy as jnp
from jax import lax
from jax.experimental import pallas as pl
from jax.experimental.pallas import tpu as pltpu
from jax.sharding import PartitionSpec as P

VMEM_BYTES = 58 * 1024 * 1024
CHUNK = 1024


def params():
    return pltpu.CompilerParams(vmem_limit_bytes=VMEM_BYTES)


def whole():
    return pl.BlockSpec(memory_space=pltpu.VMEM)


def comm_params(number):
    return pltpu.CompilerParams(
        vmem_limit_bytes=VMEM_BYTES, collective_id=number, has_side_effects=True
    )


def remote(src, dst, send, recv, axis, target):
    return pltpu.make_async_remote_copy(
        src_ref=src,
        dst_ref=dst,
        send_sem=send,
        recv_sem=recv,
        device_id={axis: target},
        device_id_type=pl.DeviceIdType.MESH,
    )


def greet(counts):
    barrier = pltpu.get_barrier_semaphore()
    for axis, count in counts:
        me = lax.axis_index(axis)
        for r in range(1, count):
            pl.semaphore_signal(
                barrier,
                inc=1,
                device_id={axis: lax.rem(me + r, count)},
                device_id_type=pl.DeviceIdType.MESH,
            )
    return barrier, sum(count - 1 for _, count in counts)


def send_kernel(
    doms, subs, slots, list_ref, own_ref, part_ref, halo_ref, outgoing, own_sems, *sems
):
    dom_send, dom_recv, sub_send, sub_recv = sems
    dom, sub = lax.axis_index("dom"), lax.axis_index("sub")
    barrier, count = greet((("dom", doms), ("sub", subs)))
    for n in range(doms * slots):
        outgoing[n // slots, n % slots] = own_ref[list_ref[n]]
    pl.semaphore_wait(barrier, count)
    copies = []
    for r in sorted(range(1, doms), key=lambda r: abs(r - doms // 2)):
        peer = lax.rem(dom + r, doms)
        copies.append(
            remote(
                outgoing.at[peer], halo_ref.at[dom], dom_send.at[r], dom_recv.at[r], "dom", peer
            )
        )
        copies[-1].start()
    for r in range(1, subs):
        peer = lax.rem(sub + r, subs)
        copies.append(
            remote(own_ref, part_ref.at[sub], sub_send.at[r], sub_recv.at[r], "sub", peer)
        )
        copies[-1].start()
    mine = (
        pltpu.make_async_copy(outgoing.at[dom], halo_ref.at[dom], own_sems.at[0]),
        pltpu.make_async_copy(own_ref, part_ref.at[sub], own_sems.at[1]),
    )
    for copy in mine:
        copy.start()
    for copy in mine:
        copy.wait()
    for copy in copies:
        copy.wait()


def send_history(own_blocks, flat_list, doms, subs, slots):
    block = own_blocks.shape[1:]
    dma = pltpu.SemaphoreType.DMA
    return pl.pallas_call(
        functools.partial(send_kernel, doms, subs, slots),
        out_shape=(
            jax.ShapeDtypeStruct((subs,) + own_blocks.shape, own_blocks.dtype),
            jax.ShapeDtypeStruct((doms, slots) + block, own_blocks.dtype),
        ),
        in_specs=[pl.BlockSpec(memory_space=pltpu.SMEM), whole()],
        out_specs=(pl.BlockSpec(memory_space=pl.ANY),) * 2,
        scratch_shapes=[
            pltpu.VMEM((doms, slots) + block, own_blocks.dtype),
            dma((2,)),
            dma((doms,)),
            dma((doms,)),
            dma((subs,)),
            dma((subs,)),
        ],
        compiler_params=comm_params(1),
        name="send_history",
    )(flat_list, own_blocks)


def return_kernel(
    doms,
    subs,
    slots,
    term_ref,
    grads_ref,
    local_ref,
    halo_ref,
    all_ref,
    quarters,
    quarter,
    pieces,
    joined,
    result,
    own_sems,
    *sems,
):
    (halo_send, halo_recv, local_send, local_recv) = sems[:4]
    (first_send, first_recv, second_send, second_recv) = sems[4:8]
    (third_send, third_recv, fourth_send, fourth_recv) = sems[8:]
    dom, sub = lax.axis_index("dom"), lax.axis_index("sub")
    blocks = local_ref.shape[1]
    part = subs * blocks
    barrier, count = greet((("dom", doms), ("sub", subs)))
    pl.semaphore_wait(barrier, count)

    def dom_peers():
        return [(r, lax.rem(dom + r, doms)) for r in range(1, doms)]

    def sub_peers():
        return [(r, lax.rem(sub + r, subs)) for r in range(1, subs)]

    def run(copies):
        for copy in copies:
            copy.start()
        return copies

    def finish_all(copies):
        for copy in copies:
            copy.wait()

    first = run(
        [
            remote(
                grads_ref.at[p], quarters.at[r], first_send.at[r], first_recv.at[r], "sub", p
            )
            for r, p in sub_peers()
        ]
    )
    big = run(
        [
            remote(
                term_ref.at[pl.ds(part + p * slots, slots)],
                halo_ref.at[pl.ds(dom * slots, slots)],
                halo_send.at[r],
                halo_recv.at[r],
                "dom",
                p,
            )
            for r, p in dom_peers()
        ]
        + [
            remote(
                term_ref.at[pl.ds(p * blocks, blocks)],
                local_ref.at[r],
                local_send.at[r],
                local_recv.at[r],
                "sub",
                p,
            )
            for r, p in sub_peers()
        ]
    )
    mine = run(
        [
            pltpu.make_async_copy(
                term_ref.at[pl.ds(part + dom * slots, slots)],
                halo_ref.at[pl.ds(dom * slots, slots)],
                own_sems.at[0],
            ),
            pltpu.make_async_copy(
                term_ref.at[pl.ds(sub * blocks, blocks)], local_ref.at[0], own_sems.at[1]
            ),
        ]
    )
    finish_all(first)
    total = grads_ref[sub]
    for r in range(1, subs):
        total += quarters[r]
    quarter[...] = total
    second = run(
        [
            remote(quarter.at[p], pieces.at[r], second_send.at[r], second_recv.at[r], "dom", p)
            for r, p in dom_peers()
        ]
    )
    finish_all(second)
    total = quarter[dom]
    for r in range(1, doms):
        total += pieces[r]
    joined[dom] = total
    third = run(
        [
            remote(
                joined.at[dom], joined.at[dom], third_send.at[r], third_recv.at[r], "dom", p
            )
            for r, p in dom_peers()
        ]
    )
    finish_all(third)
    result[sub] = joined[...]
    fourth = run(
        [
            remote(joined, result.at[sub], fourth_send.at[r], fourth_recv.at[r], "sub", p)
            for r, p in sub_peers()
        ]
    )
    finish_all(fourth)
    all_ref[...] = result[...]
    finish_all(mine)
    finish_all(big)


def return_terms(term, grads, doms, subs, slots, blocks):
    dma = pltpu.SemaphoreType.DMA
    block = term.shape[1:]
    piece = grads.shape[2:]
    counts = [doms, doms, subs, subs, subs, subs, doms, doms, doms, doms, subs, subs]
    return pl.pallas_call(
        functools.partial(return_kernel, doms, subs, slots),
        out_shape=(
            jax.ShapeDtypeStruct((subs, blocks) + block, term.dtype),
            jax.ShapeDtypeStruct((doms * slots,) + block, term.dtype),
            jax.ShapeDtypeStruct(grads.shape, grads.dtype),
        ),
        in_specs=[pl.BlockSpec(memory_space=pl.ANY), whole()],
        out_specs=(pl.BlockSpec(memory_space=pl.ANY),) * 2 + (whole(),),
        scratch_shapes=[
            pltpu.VMEM(grads.shape, grads.dtype),
            pltpu.VMEM((doms,) + piece, grads.dtype),
            pltpu.VMEM((doms,) + piece, grads.dtype),
            pltpu.VMEM((doms,) + piece, grads.dtype),
            pltpu.VMEM(grads.shape, grads.dtype),
            dma((2,)),
        ]
        + [dma((count,)) for count in counts],
        compiler_params=comm_params(2),
        name="return_terms",
    )(term, grads)


def dense_kernel(source_ref, live_ref, tile_ref, out_ref, total):
    block = pl.program_id(0)
    rows = tile_ref.shape[2]
    total[...] = jnp.zeros_like(total)

    def add(t, _):
        source = source_ref[block, t]
        total[source] += tile_ref[0, t].astype(jnp.float32)
        return 0

    lax.fori_loop(0, live_ref[block], add, 0)
    for source in range(total.shape[0]):
        out_ref[:, source * rows : (source + 1) * rows] = total[source].astype(out_ref.dtype)


def dense_adjacency(tile_source, tile_live, tile_weight, source_total):
    blocks, slots, rows, _ = tile_weight.shape
    return pl.pallas_call(
        dense_kernel,
        out_shape=jax.ShapeDtypeStruct((blocks * rows, source_total * rows), tile_weight.dtype),
        grid_spec=pltpu.PrefetchScalarGridSpec(
            num_scalar_prefetch=2,
            grid=(blocks,),
            in_specs=[pl.BlockSpec((1, slots, rows, rows), lambda b, *_: (b, 0, 0, 0))],
            out_specs=pl.BlockSpec((rows, source_total * rows), lambda b, *_: (b, 0)),
            scratch_shapes=[pltpu.VMEM((source_total, rows, rows), jnp.float32)],
        ),
        compiler_params=params(),
        cost_estimate=pl.CostEstimate(
            flops=4 * tile_weight.size, bytes_accessed=4 * tile_weight.size, transcendentals=0
        ),
        name="dense",
    )(tile_source, tile_live, tile_weight)


def layer_kernel(
    classes,
    dense_hbm,
    part_ref,
    halo_ref,
    history_ref,
    degree_ref,
    label_ref,
    neigh_ref,
    self_ref,
    term_ref,
    delta_ref,
    grads_ref,
    dense,
    total,
    scaled_t,
    sems,
):
    columns = dense.shape[1]
    chunks = columns // CHUNK
    part_rows = part_ref.shape[0]

    def fetch(c):
        return pltpu.make_async_copy(
            dense_hbm.at[:, pl.ds(c * CHUNK, CHUNK)], dense.at[:, pl.ds(c * CHUNK, CHUNK)], sems.at[c]
        )

    for c in range(chunks):
        fetch(c).start()
    for c in range(chunks):
        fetch(c).wait()
        start = c * CHUNK
        if start < part_rows:
            sources = part_ref[start : start + CHUNK, :]
        else:
            sources = halo_ref[start - part_rows : start - part_rows + CHUNK, :]
        product = jnp.dot(
            dense[:, start : start + CHUNK], sources, preferred_element_type=jnp.float32
        )
        if c == 0:
            total[...] = product
        else:
            total[...] += product
    degree = degree_ref[...].astype(jnp.float32)
    aggregate = (total[...] / degree).astype(jnp.bfloat16)
    history = history_ref[...]
    logits = jnp.dot(aggregate, neigh_ref[...], preferred_element_type=jnp.float32) + jnp.dot(
        history, self_ref[...], preferred_element_type=jnp.float32
    )
    column = lax.broadcasted_iota(jnp.int32, logits.shape, 1)
    logits = jnp.where(column < classes, logits, -jnp.inf)
    exps = jnp.exp(logits - jnp.max(logits, axis=1, keepdims=True))
    predicted = exps / jnp.sum(exps, axis=1, keepdims=True)
    residual = predicted - (column == label_ref[...]).astype(jnp.float32)
    delta_ref[...] = residual.astype(jnp.bfloat16)
    scaled_t[...] = jnp.transpose(residual / degree)[: scaled_t.shape[0]].astype(jnp.bfloat16)
    delta_t = jnp.transpose(residual).astype(jnp.bfloat16)
    width = neigh_ref.shape[1]
    grads_ref[:width, :] = jnp.dot(delta_t, aggregate, preferred_element_type=jnp.float32)
    grads_ref[width:, :] = jnp.dot(delta_t, history, preferred_element_type=jnp.float32)
    rows = term_ref.shape[2]
    step = 4 * rows
    for start in range(0, columns, step):
        term = jnp.dot(
            scaled_t[...], dense[:, start : start + step], preferred_element_type=jnp.float32
        ).astype(jnp.bfloat16)
        for i in range(4):
            term_ref[start // rows + i] = term[:, i * rows : (i + 1) * rows]


def layer(dense, part, halo, history, degree, labels, neigh, self_w, classes, rows):
    nodes, columns = dense.shape
    width = history.shape[1]
    padded = neigh.shape[1]
    short = -(-classes // 16) * 16
    return pl.pallas_call(
        functools.partial(layer_kernel, classes),
        out_shape=(
            jax.ShapeDtypeStruct((columns // rows, short, rows), jnp.bfloat16),
            jax.ShapeDtypeStruct((nodes, padded), jnp.bfloat16),
            jax.ShapeDtypeStruct((2 * padded, width), jnp.float32),
        ),
        in_specs=[pl.BlockSpec(memory_space=pl.ANY)] + [whole()] * 7,
        out_specs=(whole(),) * 3,
        scratch_shapes=[
            pltpu.VMEM((nodes, columns), jnp.bfloat16),
            pltpu.VMEM((nodes, width), jnp.float32),
            pltpu.VMEM((short, nodes), jnp.bfloat16),
            pltpu.SemaphoreType.DMA((columns // CHUNK,)),
        ],
        compiler_params=params(),
        cost_estimate=pl.CostEstimate(
            flops=4 * nodes * columns * width, bytes_accessed=2 * dense.size, transcendentals=0
        ),
        name="layer",
    )(dense, part, halo, history, degree, labels, neigh, self_w)


def finish_kernel(list_ref, local_ref, halo_ref, delta_ref, neigh_ref, self_ref, out_ref, total):
    blocks, short, rows = total.shape
    for i in range(blocks):
        value = local_ref[0, i].astype(jnp.float32)
        for s in range(1, local_ref.shape[0]):
            value += local_ref[s, i].astype(jnp.float32)
        total[i] = value

    def add(n, _):
        total[list_ref[n]] += halo_ref[n].astype(jnp.float32)
        return 0

    lax.fori_loop(0, halo_ref.shape[0], add, 0)
    neigh = neigh_ref[...]
    for i in range(blocks):
        value = total[i]
        value = jnp.transpose(
            jnp.concatenate([value, jnp.zeros((neigh.shape[1] - short, rows), jnp.float32)], axis=0)
        )
        high = value.astype(jnp.bfloat16)
        low = (value - high.astype(jnp.float32)).astype(jnp.bfloat16)
        dims = (((1,), (1,)), ((), ()))
        out = lax.dot_general(high, neigh, dims, preferred_element_type=jnp.float32)
        out += lax.dot_general(low, neigh, dims, preferred_element_type=jnp.float32)
        out += lax.dot_general(
            delta_ref[i * rows : (i + 1) * rows, :],
            self_ref[...],
            dims,
            preferred_element_type=jnp.float32,
        )
        out_ref[i * rows : (i + 1) * rows, :] = out


def finish(flat_list, local, halo, delta, neigh, self_w):
    blocks, short, rows = local.shape[1:]
    return pl.pallas_call(
        finish_kernel,
        out_shape=jax.ShapeDtypeStruct((delta.shape[0], neigh.shape[0]), jnp.float32),
        in_specs=[pl.BlockSpec(memory_space=pltpu.SMEM)] + [whole()] * 5,
        out_specs=whole(),
        scratch_shapes=[pltpu.VMEM((blocks, short, rows), jnp.float32)],
        compiler_params=params(),
        name="finish",
    )(flat_list, local, halo, delta, neigh, self_w)


def per_device(
    history,
    tile_weight,
    tile_source,
    tile_live,
    send_list,
    degree,
    labels,
    neigh_weight,
    self_weight,
):
    block_count, _, rows, _ = tile_weight.shape
    width = history.shape[1]
    classes = neigh_weight.shape[1]
    dom_count, sub_count = lax.axis_size("dom"), lax.axis_size("sub")
    devices = dom_count * sub_count
    slots = send_list.shape[2]
    part_blocks = block_count * sub_count
    source_total = part_blocks + dom_count * slots
    nodes_all = history.shape[0] * devices
    flat_list = send_list.reshape(-1)
    own_blocks = history.reshape(block_count, rows, width)
    part, halo = send_history(own_blocks, flat_list, dom_count, sub_count, slots)
    dense = dense_adjacency(tile_source, tile_live, tile_weight, source_total)
    pad = ((0, 0), (0, -classes % 128))
    neigh = jnp.pad(neigh_weight, pad)
    self_w = jnp.pad(self_weight, pad)
    padded = neigh.shape[1]
    term, delta, grads = layer(
        dense,
        part.reshape(-1, width),
        halo.reshape(-1, width),
        history,
        degree[:, None],
        labels[:, None],
        neigh,
        self_w,
        classes,
        rows,
    )
    pieces = (sub_count, dom_count, 2 * padded // devices, width)
    local_back, halo_back, grads_all = return_terms(
        term, grads.reshape(pieces), dom_count, sub_count, slots, block_count
    )
    grads_all = grads_all.reshape(2, padded, width)[:, :classes].transpose(0, 2, 1)
    grads_all = grads_all * float(nodes_all) ** (-0.5)
    grad_history = finish(
        flat_list,
        local_back,
        halo_back,
        delta,
        neigh,
        self_w,
    )
    return (grad_history, grads_all[0], grads_all[1])


def solution(mesh):
    placed = (
        P(("dom", "sub"), None),
        P(("dom", "sub"), None, None, None),
        P(("dom", "sub"), None),
        P(("dom", "sub")),
        P(("dom", "sub"), None, None),
        P(("dom", "sub")),
        P(("dom", "sub")),
        P(),
        P(),
    )
    return jax.shard_map(
        per_device,
        mesh=mesh,
        in_specs=placed,
        out_specs=(P(("dom", "sub"), None), P(), P()),
        check_vma=False,
    )
```

time: 386 us -> 159 us (0.41)
  waiting for transfers between devices: 192 us -> 0 us
  Pallas kernels: 0 us -> 149 us
  matrix products: 116 us -> 0 us
  local copies, waits for them, and re-layouts: 48 us -> 8.91 us
  between operations: 14 us -> 0.68 us
  starting transfers between devices: 11.2 us -> 0 us
    pallas_call x0 -> x5, Pallas kernels: none -> 149 us  [the longest x1 61.1 us: return_terms(): pl.pallas_call(functools.partial(return_kernel, doms, subs, slots), out_s...]
    psum x1 -> x0, waiting for transfers between devices: 144 us -> none  [per_device(): neigh_total, self_total = lax.psum((neigh_part, self_part), ('dom', 'sub'))]
    dot_general x12 -> x0, matrix products: 116 us -> none  [the longest x1 62 us: per_device(): jnp.einsum('bts,btjc->sjc', picker.astype(jnp.float32), per_tile, precisi...]
    unnamed x4 -> x0, waiting for transfers between devices: 28.7 us -> none
    unnamed x30 -> x5, local copies, waits for them, and re-layouts: 28.8 us -> 2.73 us
    all_to_all x2 -> x0, waiting for transfers between devices: 16.2 us -> none  [the longest x1 16.2 us: per_device(): lax.all_to_all(outgoing, 'dom', split_axis=0, concat_axis=0, tiled=True)]
    all_to_all x2 -> x0, starting transfers between devices: 11.1 us -> none  [the longest x1 6.39 us: per_device(): lax.all_to_all(outgoing, 'dom', split_axis=0, concat_axis=0, tiled=True)]
    reshape x3 -> x1, local copies, waits for them, and re-layouts: 8.32 us -> 0.62 us  [per_device(): flat_list = send_list.reshape(-1)]
  transfers between devices with their start and end apart: 5 -> 0, of which waited for: 4 -> 0; matrix products, arithmetic and copies ran while one was open for 10% -> 0% of each run, Pallas kernels for 0% -> 0%
where the time goes in v1:
time: 159 us
  Pallas kernels  149 us (94%)
  local copies, waits for them, and re-layouts  8.91 us (6%)
    pallas_call x1, Pallas kernels, return_terms(): pl.pallas_call(functools.partial(return_kernel, doms, subs, slots), out_s...  61.1 us
    pallas_call x1, Pallas kernels, send_history(): pl.pallas_call(functools.partial(send_kernel, doms, subs, slots), out_sha...  43.4 us
    pallas_call x1, Pallas kernels, layer(): pl.pallas_call(functools.partial(layer_kernel, classes), out_shape=(jax.S...  21.8 us
    pallas_call x1, Pallas kernels, dense_adjacency(): pl.pallas_call(dense_kernel, out_shape=jax.ShapeDtypeStruct((blocks * row...  18.1 us
    pallas_call x1, Pallas kernels, finish(): pl.pallas_call(finish_kernel, out_shape=jax.ShapeDtypeStruct((delta.shape...  4.77 us

profile of v1, /device:TPU:1, one launch (start us, length us, event | category | flops | bytes accessed | tf_op | source)
XLA Modules:
  0.0 158.7 jit_solution(7993346050440637561)
XLA Ops:
  0.6 0.8 copy.15
  1.4 0.6 reshape.24.list_ref
  2.0 1.0 copy.16
  3.0 0.7 pad.7.neigh_ref
  3.7 1.0 copy.17
  4.7 0.7 pad.8.self_ref
  5.3 1.7 %copy.18.degree_ref = s32[1024,1]{1,0:T(8,128)} copy(s32[1024,1]{0,1:T(1,128)} %bitcast.16) | data formatting | bytes 8192 | tf_op jit(solution)/shard_map/broadcast_in_dim | solution.py:476
  7.1 1.7 %copy.19.label_ref = s32[1024,1]{1,0:T(8,128)} copy(s32[1024,1]{0,1:T(1,128)} %bitcast.17) | data formatting | bytes 8192 | tf_op jit(solution)/shard_map/broadcast_in_dim | solution.py:477
  8.8 43.4 %send_history.1 = (bf16[4,8,128,256]{3,2,1,0:T(8,128)(2,1)}, bf16[8,4,128,256]{3,2,1,0:T(8,128)(2,1)}) custom-call(s32[32]{0:T(128)} %reshape.24.list_ref, bf16[8,128,256]{2,1,0:T(8,128)(2,1)} %bitcast.13), custom_call_target="tpu_custom_call" | custom-call | tf_op jit(solution)/shard_map/send_history/pallas_call | solution.py:92
  52.2 18.1 %dense.1.dense_hbm = bf16[1024,8192]{1,0:T(8,128)(2,1)} custom-call(s32[8,64]{1,0:T(8,128)} %source_ref.1, s32[8]{0:T(128)} %live_ref.1, bf16[8,64,128,128]{3,2,1,0:T(8,128)(2,1)} %tile_ref.1), custom_call_target="tpu_custom_call" | custom-call | flops 33554432 | bytes 33554432 | tf_op jit(solution)/shard_map/dense/pallas_call | solution.py:281
  70.3 21.8 %layer.1 = (bf16[64,176,128]{2,1,0:T(8,128)(2,1)}, bf16[1024,256]{1,0:T(8,128)(2,1)}, f32[512,256]{1,0:T(8,128)}) custom-call(bf16[1024,8192]{1,0:T(8,128)(2,1)} %dense.1.dense_hbm, bf16[4096,256]{1,0:T(8,128)(2,1)} %bitcast.18, bf16[4096,256]{1,0:T(8,128)(2,1)} %bitcast.19, bf16[1024,256]{1,0:T(8,128)(2,1)} %history_ref.1, s32[1024,1]{1,0:T(8,128)} %copy.18.degree_ref, ...), custom_call_target="tpu_custom_call" | custom-call | flops 8589934592 | bytes 16777216 | tf_op jit(solution)/shard_map/layer/pallas_call | solution.py:374
  92.1 61.1 %return_terms.1 = (bf16[4,8,176,128]{3,2,1,0:T(8,128)(2,1)}, bf16[32,176,128]{2,1,0:T(8,128)(2,1)}, f32[4,8,16,256]{3,2,1,0:T(8,128)}) custom-call(bf16[64,176,128]{2,1,0:T(8,128)(2,1)} %get-tuple-element.13.term_ref, f32[4,8,16,256]{3,2,1,0:T(8,128)} %bitcast.14), custom_call_target="tpu_custom_call" | custom-call | tf_op jit(solution)/shard_map/return_terms/pallas_call | solution.py:241
  153.2 0.0 copy-start
  153.2 4.8 %finish.1 = f32[1024,256]{1,0:T(8,128)} custom-call(s32[32]{0:T(128)} %reshape.24.list_ref, bf16[4,8,176,128]{3,2,1,0:T(8,128)(2,1)} %get-tuple-element.15.local_ref, bf16[32,176,128]{2,1,0:T(8,128)(2,1)} %get-tuple-element.16.halo_ref, bf16[1024,256]{1,0:T(8,128)(2,1)} %get-tuple-element.17.delta_ref, bf16[256,256]{1,0:T(8,128)(2,1)} %pad.7.neigh_ref, ...), custom_call_target="tpu_custom_call" | custom-call | tf_op jit(solution)/shard_map/finish/pallas_call | solution.py:432
  157.9 0.0 copy-done
  158.0 0.8 slice_bitcast_fusion
  (1 shorter events, 0.0 us)
Async XLA Ops:
  153.2 4.8 %copy-start = (f32[4,8,16,256]{3,2,1,0:T(8,128)S(1)}, f32[4,8,16,256]{3,2,1,0:T(8,128)}, u32[]{:S(2)}) copy-start(f32[4,8,16,256]{3,2,1,0:T(8,128)} %get-tuple-element.18) | copy-start | bytes 1572868

commit v2 on v1

--- a/solution.py
+++ b/solution.py
@@ -296,6 +296,15 @@
     )(tile_source, tile_live, tile_weight)
 
 
+def as_column(ref):
+    rows = ref.shape[1]
+    parts = [
+        jnp.transpose(jnp.broadcast_to(ref[i : i + 1, :].astype(jnp.float32), (rows, rows)))
+        for i in range(ref.shape[0])
+    ]
+    return jnp.concatenate(parts, axis=0)[:, :1]
+
+
 def layer_kernel(
     classes,
     dense_hbm,
@@ -339,7 +348,7 @@
             total[...] = product
         else:
             total[...] += product
-    degree = degree_ref[...].astype(jnp.float32)
+    degree = as_column(degree_ref)
     aggregate = (total[...] / degree).astype(jnp.bfloat16)
     history = history_ref[...]
     logits = jnp.dot(aggregate, neigh_ref[...], preferred_element_type=jnp.float32) + jnp.dot(
@@ -349,7 +358,7 @@
     logits = jnp.where(column < classes, logits, -jnp.inf)
     exps = jnp.exp(logits - jnp.max(logits, axis=1, keepdims=True))
     predicted = exps / jnp.sum(exps, axis=1, keepdims=True)
-    residual = predicted - (column == label_ref[...]).astype(jnp.float32)
+    residual = predicted - (column == as_column(label_ref).astype(jnp.int32)).astype(jnp.float32)
     delta_ref[...] = residual.astype(jnp.bfloat16)
     scaled_t[...] = jnp.transpose(residual / degree)[: scaled_t.shape[0]].astype(jnp.bfloat16)
     delta_t = jnp.transpose(residual).astype(jnp.bfloat16)
@@ -357,12 +366,12 @@
     grads_ref[:width, :] = jnp.dot(delta_t, aggregate, preferred_element_type=jnp.float32)
     grads_ref[width:, :] = jnp.dot(delta_t, history, preferred_element_type=jnp.float32)
     rows = term_ref.shape[2]
-    step = 4 * rows
+    step = 8 * rows
     for start in range(0, columns, step):
         term = jnp.dot(
             scaled_t[...], dense[:, start : start + step], preferred_element_type=jnp.float32
         ).astype(jnp.bfloat16)
-        for i in range(4):
+        for i in range(8):
             term_ref[start // rows + i] = term[:, i * rows : (i + 1) * rows]
 
 
@@ -473,8 +482,8 @@
         part.reshape(-1, width),
         halo.reshape(-1, width),
         history,
-        degree[:, None],
-        labels[:, None],
+        degree.reshape(block_count, rows),
+        labels.reshape(block_count, rows),
         neigh,
         self_w,
         classes,

time: 159 us -> 154 us (0.969)
  local copies, waits for them, and re-layouts: 8.91 us -> 5.49 us
    broadcast_in_dim x2 -> x0, local copies, waits for them, and re-layouts: 3.45 us -> none  [the longest x1 1.75 us: per_device(): labels[:, None]]
where the time goes in v2:
time: 154 us
  Pallas kernels  148 us (96%)
  local copies, waits for them, and re-layouts  5.49 us (4%)
    pallas_call x1, Pallas kernels, return_terms(): pl.pallas_call(functools.partial(return_kernel, doms, subs, slots), out_s...  59.7 us
    pallas_call x1, Pallas kernels, send_history(): pl.pallas_call(functools.partial(send_kernel, doms, subs, slots), out_sha...  43.4 us
    pallas_call x1, Pallas kernels, layer(): pl.pallas_call(functools.partial(layer_kernel, classes), out_shape=(jax.S...  21.7 us
    pallas_call x1, Pallas kernels, dense_adjacency(): pl.pallas_call(dense_kernel, out_shape=jax.ShapeDtypeStruct((blocks * row...  18 us
    pallas_call x1, Pallas kernels, finish(): pl.pallas_call(finish_kernel, out_shape=jax.ShapeDtypeStruct((delta.shape...  4.77 us

profile of v2, /device:TPU:1, one launch (start us, length us, event | category | flops | bytes accessed | tf_op | source)
XLA Modules:
  0.0 153.8 jit_solution(5488800480402276028)
XLA Ops:
  0.6 0.8 copy.15
  1.4 0.6 reshape.30.list_ref
  2.0 1.0 copy.16
  3.0 0.7 pad.7.neigh_ref
  3.7 1.0 copy.17
  4.7 0.7 pad.8.self_ref
  5.4 43.4 %send_history.1 = (bf16[4,8,128,256]{3,2,1,0:T(8,128)(2,1)}, bf16[8,4,128,256]{3,2,1,0:T(8,128)(2,1)}) custom-call(s32[32]{0:T(128)} %reshape.30.list_ref, bf16[8,128,256]{2,1,0:T(8,128)(2,1)} %bitcast.13), custom_call_target="tpu_custom_call" | custom-call | tf_op jit(solution)/shard_map/send_history/pallas_call | solution.py:92
  48.8 18.0 %dense.1.dense_hbm = bf16[1024,8192]{1,0:T(8,128)(2,1)} custom-call(s32[8,64]{1,0:T(8,128)} %source_ref.1, s32[8]{0:T(128)} %live_ref.1, bf16[8,64,128,128]{3,2,1,0:T(8,128)(2,1)} %tile_ref.1), custom_call_target="tpu_custom_call" | custom-call | flops 33554432 | bytes 33554432 | tf_op jit(solution)/shard_map/dense/pallas_call | solution.py:281
  66.8 21.7 %layer.1 = (bf16[64,176,128]{2,1,0:T(8,128)(2,1)}, bf16[1024,256]{1,0:T(8,128)(2,1)}, f32[512,256]{1,0:T(8,128)}) custom-call(bf16[1024,8192]{1,0:T(8,128)(2,1)} %dense.1.dense_hbm, bf16[4096,256]{1,0:T(8,128)(2,1)} %bitcast.16, bf16[4096,256]{1,0:T(8,128)(2,1)} %bitcast.17, bf16[1024,256]{1,0:T(8,128)(2,1)} %history_ref.1, s32[8,128]{1,0:T(8,128)} %bitcast.18, ...), custom_call_target="tpu_custom_call" | custom-call | flops 8589934592 | bytes 16777216 | tf_op jit(solution)/shard_map/layer/pallas_call | solution.py:383
  88.5 59.7 %return_terms.1 = (bf16[4,8,176,128]{3,2,1,0:T(8,128)(2,1)}, bf16[32,176,128]{2,1,0:T(8,128)(2,1)}, f32[4,8,16,256]{3,2,1,0:T(8,128)}) custom-call(bf16[64,176,128]{2,1,0:T(8,128)(2,1)} %get-tuple-element.13.term_ref, f32[4,8,16,256]{3,2,1,0:T(8,128)} %bitcast.14), custom_call_target="tpu_custom_call" | custom-call | tf_op jit(solution)/shard_map/return_terms/pallas_call | solution.py:241
  148.2 0.0 copy-start
  148.2 4.8 %finish.1 = f32[1024,256]{1,0:T(8,128)} custom-call(s32[32]{0:T(128)} %reshape.30.list_ref, bf16[4,8,176,128]{3,2,1,0:T(8,128)(2,1)} %get-tuple-element.15.local_ref, bf16[32,176,128]{2,1,0:T(8,128)(2,1)} %get-tuple-element.16.halo_ref, bf16[1024,256]{1,0:T(8,128)(2,1)} %get-tuple-element.17.delta_ref, bf16[256,256]{1,0:T(8,128)(2,1)} %pad.7.neigh_ref, ...), custom_call_target="tpu_custom_call" | custom-call | tf_op jit(solution)/shard_map/finish/pallas_call | solution.py:441
  153.0 0.0 copy-done
  153.0 0.8 slice_bitcast_fusion
  (1 shorter events, 0.0 us)
Async XLA Ops:
  148.2 4.8 %copy-start = (f32[4,8,16,256]{3,2,1,0:T(8,128)S(1)}, f32[4,8,16,256]{3,2,1,0:T(8,128)}, u32[]{:S(2)}) copy-start(f32[4,8,16,256]{3,2,1,0:T(8,128)} %get-tuple-element.18) | copy-start | bytes 1572868
